TPU v7x, 512 devices: a whole 4x4x16 slice. The times are simulated.
512 devices in a mesh: dp: 32 (over y, x, core), group: 2 (over z_hi), tensor: 8 (over z_lo).
Axes of the slice: x: 4, y: 4, z: 16 (z_hi: 2, z_lo: 8; z = z_hi * 8 + z_lo), core: 2. Of those that a mesh axis runs over, the one named last changes fastest.
Arguments:
- teacher_hidden: bfloat16 [256, 4608], P('dp', ('group', 'tensor')), may hold values from -6 to 6
- student_hidden: bfloat16 [256, 3584], P('dp', ('group', 'tensor')), may hold values from -6 to 6
- teacher_gain: bfloat16 [4608], replicated, may hold values from 0.099609375 to 1.8984375
- student_gain: bfloat16 [3584], replicated, may hold values from 0.099609375 to 1.8984375
- teacher_unembed: bfloat16 [131072, 4608], P(('dp', 'group', 'tensor')), may hold values from -0.25 to 0.25
- student_unembed: bfloat16 [131072, 3584], P(('dp', 'group', 'tensor')), may hold values from -0.3125 to 0.3125
- labels: int32 [256], replicated, may hold values from 0 to 131071
Outputs:
- token_loss: float32 [256], P('dp')
- student_grad: bfloat16 [256, 3584], P('dp', ('group', 'tensor'))
All inputs are finite; a program needn't handle non-finite values.
Results may differ from a plain program's by a relative error of at most 0.0055.
Values may be sent and summed in bfloat16 or wider, within the bound.
A program may use at most 64 MiB of HBM per device.

v0:
```python
import jax
import jax.numpy as jnp
from jax import lax
from jax.sharding import PartitionSpec as P

SOFT_CAP = 30.0
EPSILON = 1e-06


def normalize(hidden, gain_vector):
    values = hidden.astype(jnp.float32)
    inverse = lax.rsqrt(jnp.mean(values * values, axis=1) + EPSILON)
    scaled = (values * inverse[:, None] * gain_vector.astype(jnp.float32)).astype(jnp.bfloat16)
    return (scaled, inverse)


def project_rows(left, weight):
    return lax.dot_general(
        left, weight, (((1,), (1,)), ((), ())), preferred_element_type=jnp.float32
    )


def on_device(
    teacher_hidden,
    student_hidden,
    teacher_gain,
    student_gain,
    teacher_unembed,
    student_unembed,
    labels,
):
    tok_dev = teacher_hidden.shape[0]
    teacher_local = teacher_hidden.shape[1]
    student_local = student_hidden.shape[1]
    lane_count = lax.axis_size(("group", "tensor"))
    teacher_width = teacher_local * lane_count
    student_width = student_local * lane_count
    vocab_local = teacher_unembed.shape[0]
    row_owner = lax.axis_index("dp")
    lane_index = lax.axis_index(("group", "tensor"))
    full_teacher, full_student = (
        lax.all_gather(teacher_hidden, ("group", "tensor"), axis=1, tiled=True),
        lax.all_gather(student_hidden, ("group", "tensor"), axis=1, tiled=True),
    )
    scaled_teacher, inv_unused = normalize(full_teacher, teacher_gain)
    scaled_student, inv_student = normalize(full_student, student_gain)
    scaled_rows = jnp.concatenate([scaled_teacher, scaled_student], axis=1)
    shard_piece = lax.all_gather(scaled_rows, "dp", axis=0, tiled=True)
    raw_logits = jnp.concatenate(
        [
            project_rows(shard_piece[:, :teacher_width], teacher_unembed),
            project_rows(shard_piece[:, teacher_width:], student_unembed),
        ],
        axis=1,
    )
    raw_teacher = raw_logits[:, :vocab_local]
    raw_student = raw_logits[:, vocab_local:]
    logit_teacher = SOFT_CAP * jnp.tanh(raw_teacher / SOFT_CAP)
    logit_student = SOFT_CAP * jnp.tanh(raw_student / SOFT_CAP)
    exp_teacher = jnp.exp(logit_teacher)
    exp_student = jnp.exp(logit_student)
    vocab_start = lax.axis_index(("dp", "group", "tensor")) * vocab_local
    vocab_ids = vocab_start + jnp.arange(vocab_local, dtype=jnp.int32)
    onehot = labels[:, None] == vocab_ids[None, :]
    sum_teacher, sum_student, cross, picked = lax.psum(
        (
            jnp.sum(exp_teacher, axis=1),
            jnp.sum(exp_student, axis=1),
            jnp.sum(exp_teacher * (logit_teacher - logit_student), axis=1),
            jnp.sum(jnp.where(onehot, logit_student, 0.0), axis=1),
        ),
        ("dp", "group", "tensor"),
    )
    loss_all = cross / sum_teacher - jnp.log(sum_teacher) + 2.0 * jnp.log(sum_student) - picked
    token_loss = lax.dynamic_slice_in_dim(loss_all, row_owner * tok_dev, tok_dev)
    slope = 1.0 - (logit_student / SOFT_CAP) ** 2
    grad_logits = (
        2.0 * exp_student / sum_student[:, None]
        - exp_teacher / sum_teacher[:, None]
        - onehot.astype(jnp.float32)
    ) * slope
    grad_round = grad_logits.astype(jnp.bfloat16)
    radial_all = lax.psum(jnp.sum(grad_logits * raw_student, axis=1), ("dp", "group", "tensor"))
    grad_terms = jnp.dot(grad_round, student_unembed, preferred_element_type=jnp.float32)
    col_sums = lax.psum_scatter(grad_terms, ("group", "tensor"), scatter_dimension=1, tiled=True)
    back = lax.psum_scatter(col_sums, "dp", scatter_dimension=0, tiled=True)
    radial = lax.dynamic_slice_in_dim(radial_all, row_owner * tok_dev, tok_dev)
    gain_values = lax.dynamic_slice_in_dim(
        student_gain, lane_index * student_local, student_local
    ).astype(jnp.float32)
    values = student_hidden.astype(jnp.float32)
    student_grad = (
        inv_student[:, None] * gain_values[None, :] * back
        - (inv_student * inv_student * radial)[:, None] * values / student_width
    )
    return (token_loss, student_grad.astype(jnp.bfloat16))


def solution(mesh):
    in_specs = (
        P("dp", ("group", "tensor")),
        P("dp", ("group", "tensor")),
        P(),
        P(),
        P(("dp", "group", "tensor"), None),
        P(("dp", "group", "tensor"), None),
        P(),
    )
    out_specs = (P("dp"), P("dp", ("group", "tensor")))
    return jax.shard_map(
        on_device, mesh=mesh, in_specs=in_specs, out_specs=out_specs, check_vma=False
    )
```

profile of v0, /device:TPU:32, one launch (start us, length us, event | category | flops | bytes accessed | tf_op | source)
XLA Modules:
  0.0 450.2 jit_solution(14072221526141389863)
XLA Ops:
  7.2 34.0 %all-gather.1 = bf16[16,224,8]{1,2,0:T(8,128)(2,1)S(1)} all-gather(bf16[1,224,8]{1,2,0:T(8,128)(2,1)} %bitcast.18), channel_id=1, replica_groups=mesh['dp'=32,'group'=2,'tensor'=8] {'group','tensor'}, dimensions={0}, use_global_device_ids=true | all-gather | bytes 60928 | tf_op jit(solution)/shard_map/all_gather | solution.py:43
  41.2 0.1 reshape.30
  41.3 0.1 multiply_reduce_fusion.3
  41.5 0.7 convert_element_type.37
  42.2 28.9 %all-gather = bf16[16,288,8]{1,2,0:T(8,128)(2,1)S(1)} all-gather(bf16[1,288,8]{1,2,0:T(8,128)(2,1)} %bitcast.19), channel_id=1, replica_groups=mesh['dp'=32,'group'=2,'tensor'=8] {'group','tensor'}, dimensions={0}, use_global_device_ids=true | all-gather | bytes 78336 | tf_op jit(solution)/shard_map/all_gather | solution.py:42
  71.1 0.1 reshape.29
  71.2 0.2 multiply_reduce_fusion.2
  71.4 0.7 convert_element_type.34
  72.1 0.1 fusion.19
  72.2 0.1 fusion.18
  72.3 0.7 pad_maximum_fusion
  73.0 58.0 %all-gather.4.cloned.1.call-done = bf16[256,8192]{1,0:T(8,128)(2,1)} async-done(((bf16[8,8192]{1,0:T(8,128)(2,1)}), bf16[256,8192]{1,0:T(8,128)(2,1)}) %all-gather.4.cloned.1.call-update) | async-done | bytes 4194320 | tf_op jit(solution)/shard_map/all_gather | solution.py:48
  131.0 2.6 exponential_reduce_fusion.1
  133.7 2.2 exponential_reduce_fusion
  135.9 102.7 %all-reduce.1 = (f32[256]{0:T(256)S(1)}, f32[256]{0:T(256)S(1)}) all-reduce(f32[256]{0:T(256)S(1)} %get-tuple-element.16, f32[256]{0:T(256)S(1)} %get-tuple-element.18), channel_id=1, replica_groups=mesh['dp'=32,'group'=2,'tensor'=8] {'dp','group','tensor'}, use_global_device_ids=true, to_apply=%region_5.6 | all-reduce | flops 512 | bytes 4096 | tf_op jit(solution)/shard_map/psum | solution.py:65
  238.6 4.3 fusion.16
  243.0 0.8 dynamic-slice_convert_fusion
  243.7 0.3 multiply_reduce_fusion
  244.0 101.9 %all-reduce = (f32[256]{0:T(256)S(1)}, f32[256]{0:T(256)S(1)}, f32[256]{0:T(256)S(1)}) all-reduce(f32[256]{0:T(256)S(1)} %get-tuple-element.10, f32[256]{0:T(256)S(1)} %get-tuple-element.9, f32[256]{0:T(256)S(1)} %get-tuple-element.8), channel_id=1, replica_groups=mesh['dp'=32,'group'=2,'tensor'=8] {'dp','group','tensor'}, use_global_device_ids=true, to_apply=%region_9.10 | all-reduce | flops 768 | bytes 6144 | tf_op jit(solution)/shard_map/psum | solution.py:65
  345.9 1.8 copy.31
  347.7 0.6 dynamic_slice.9
  348.3 0.1 dynamic-slice_multiply_fusion
  348.4 93.9 %reduce-scatter.7.cloned.1.call-done = f32[8,224]{1,0:T(8,128)} async-done(((f32[256,224]{1,0:T(8,128)}), f32[8,224]{1,0:T(8,128)}) %reduce-scatter.7.cloned.1.call-update) | async-done | bytes 7184 | tf_op jit(solution)/shard_map/reduce_scatter | solution.py:86
  442.3 1.4 subtract_convert_fusion
  (21 shorter events, 0.3 us)
Async XLA Ops:
  7.2 123.9 %copy-start = (bf16[256,4608]{1,0:T(8,128)(2,1)S(1)}, bf16[256,4608]{1,0:T(8,128)(2,1)}, u32[]{:S(2)}) copy-start(bf16[256,4608]{1,0:T(8,128)(2,1)} %param.11) | copy-start | bytes 7077892
  7.2 123.8 %all-gather.4.cloned.1.call-start = ((), (), s32[]{:S(2)}) async-start(), calls=%async_computation.2 | async-start | bytes 4325376 | tf_op jit(solution)/shard_map/all_gather | solution.py:48
  72.9 273.0 %reduce-scatter.5.cloned.1.call-start = ((), (), s32[]{:S(2)}) async-start(), calls=%async_computation.3 | async-start | bytes 3899392 | tf_op jit(solution)/shard_map/reduce_scatter | solution.py:85
  131.0 2.6 copy-start.1
  133.7 104.9 %copy-start.3 = (s32[256]{0:T(256)S(1)}, s32[256]{0:T(256)}, u32[]{:S(2)}) copy-start(s32[256]{0:T(256)} %param.13) | copy-start | bytes 3076
  242.9 199.5 %copy-start.2 = (bf16[8,224]{1,0:T(8,128)(2,1)S(1)}, bf16[8,224]{1,0:T(8,128)(2,1)}, u32[]{:S(2)}) copy-start(bf16[8,224]{1,0:T(8,128)(2,1)} %param.8) | copy-start | bytes 10756
  242.9 199.4 %reduce-scatter.7.cloned.1.call-start = ((), (), s32[]{:S(2)}) async-start(), calls=%async_computation.4 | async-start | bytes 270336 | tf_op jit(solution)/shard_map/reduce_scatter | solution.py:86
Sparse Core Ops, SparseCore 0:
  73.1 57.9 all-gather.3
  243.0 74.9 reduce-scatter.4
  347.8 94.4 reduce-scatter.6
where the time goes:
time: 451 us; the launch traced here: 450 us
  blocking collectives  267 us (59%)
  waiting for transfers between devices  152 us (34%)
  between operations  13.8 us (3%)
  matrix products  9.12 us (2%)
  other arithmetic  5.04 us (1%)
    psum x2, blocking collectives, on_device(): lax.psum((jnp.sum(exp_teacher, axis=1), jnp.sum(exp_student, axis=1), jnp...  205 us
    reduce_scatter x1, waiting for transfers between devices, on_device(): back = lax.psum_scatter(col_sums, 'dp', scatter_dimension=0, tiled=True)  93.9 us
    all_gather x1, waiting for transfers between devices, on_device(): shard_piece = lax.all_gather(scaled_rows, 'dp', axis=0, tiled=True)  58 us
    all_gather x1, blocking collectives, on_device(): lax.all_gather(student_hidden, ('group', 'tensor'), axis=1, tiled=True)  34 us
    all_gather x1, blocking collectives, on_device(): lax.all_gather(teacher_hidden, ('group', 'tensor'), axis=1, tiled=True)  28.9 us
  transfers between devices with their start and end apart: 3, of which 2 were waited for; matrix products, arithmetic and copies ran while one was open for 0% of the time, Pallas kernels for 0%

commit v1 on v0

v1 whole, which is shorter than its diff:
```python
import jax
import jax.numpy as jnp
from jax import lax
from jax.experimental import pallas as pl
from jax.experimental.pallas import tpu as pltpu
from jax.sharding import PartitionSpec as P

CAP = 30.0
EPS = 1e-06
MESH = pl.DeviceIdType.MESH
F32 = jnp.float32
BF16 = jnp.bfloat16
RX, RY, RZ = 4, 4, 16
PLANE = RX * RY
NT = (((1,), (1,)), ((), ()))


def kernel(
    th_ref, sh_ref, tg_ref, sg_ref, lab_ref, wt_hbm, ws_hbm,
    grad_ref, loss_ref,
    wt, ws, zbuf, t0, t1, s0, s1, xt, xs, raw_t, raw_s, es_s, et_s, oh_s,
    sxy, sz, gbuf, obuf, rbuf, zsend, zrecv, cols,
    w_send, w_recv, w_loc, z_send, z_recv, g_send, g_recv,
    a_send, a_recv, b_send, b_recv, r_send, r_recv, q_send, q_recv,
):
    dp = lax.axis_index("dp")
    z = lax.axis_index("group") * 8 + lax.axis_index("tensor")
    core = dp % 2
    p = dp // 2
    x = p % RX
    y = p // RX
    tl = th_ref.shape[1]
    sl = sh_ref.shape[1]
    dt = tl * RZ
    ds = sl * RZ
    vloc = wt_hbm.shape[0]

    def at_plane(q):
        return (q * 2 + core, lax.axis_index("group"), lax.axis_index("tensor"))

    def at_line(k):
        return (dp, k // 8, k % 8)

    partner = (p * 2 + 1 - core, lax.axis_index("group"), lax.axis_index("tensor"))

    def remote(src, dst, send, recv, device):
        return pltpu.make_async_remote_copy(
            src_ref=src, dst_ref=dst, send_sem=send, recv_sem=recv,
            device_id=device, device_id_type=MESH,
        )

    own = jnp.concatenate(
        [th_ref[...].astype(F32), sh_ref[...].astype(F32)], axis=1
    )
    zbuf[z] = own.astype(BF16)

    barrier = pltpu.get_barrier_semaphore()

    @pl.loop(1, RZ)
    def _(k):
        pl.semaphore_signal(
            barrier, inc=1, device_id=at_line((z + k) % RZ), device_id_type=MESH
        )
        pl.semaphore_signal(
            barrier, inc=1, device_id=at_plane((p + k) % PLANE), device_id_type=MESH
        )

    pl.semaphore_signal(barrier, inc=1, device_id=partner, device_id_type=MESH)
    pl.semaphore_wait(barrier, 31)

    def z_copy(k, slot):
        return remote(
            zbuf.at[z], zbuf.at[slot], z_send.at[k], z_recv.at[slot],
            at_line((z + k) % RZ),
        )

    @pl.loop(1, RZ)
    def _(k):
        z_copy(k, z).start()

    w_copies = [
        remote(wt_hbm, wt.at[core], w_send.at[0], w_recv.at[0], partner),
        remote(ws_hbm, ws.at[core], w_send.at[1], w_recv.at[1], partner),
    ]
    l_copies = [
        pltpu.make_async_copy(wt_hbm, wt.at[core], w_loc.at[0]),
        pltpu.make_async_copy(ws_hbm, ws.at[core], w_loc.at[1]),
    ]
    for copy in w_copies + l_copies:
        copy.start()

    lane = lax.broadcasted_iota(jnp.int32, (8, 128), 1)
    label_row = jnp.zeros((8, 128), jnp.int32)
    for q in range(PLANE):
        row = jnp.broadcast_to(lab_ref[q // 8 : q // 8 + 1, :], (8, 128))
        shift = (8 * q - 16 * (q % 8) - 8 * core + 256) % 128
        label_row = jnp.where(lane // 8 == q, pltpu.roll(row, shift, 1), label_row)
    labels = label_row[:1, :]

    @pl.loop(1, RZ)
    def _(k):
        z_copy(k, (z + k) % RZ).wait_recv()

    pieces = [zbuf[k].astype(F32) for k in range(RZ)]
    full_t = jnp.concatenate([v[:, :tl] for v in pieces], axis=1)
    full_s = jnp.concatenate([v[:, tl:] for v in pieces], axis=1)

    def scaled(values, gain):
        inv = lax.rsqrt(jnp.sum(values * values, axis=1, keepdims=True) / values.shape[1] + EPS)
        return values * inv * gain, inv

    gain_s = sg_ref[...].astype(F32)
    sc_t, _ = scaled(full_t, tg_ref[...].astype(F32))
    sc_s, inv_s = scaled(full_s, gain_s)
    t0[p] = sc_t[:, : dt // 2].astype(BF16)
    t1[p] = sc_t[:, dt // 2 :].astype(BF16)
    s0[p] = sc_s[:, : ds // 2].astype(BF16)
    s1[p] = sc_s[:, ds // 2 :].astype(BF16)

    def make_ring(c, buf, x_first, forward):
        me1, me2 = (x, y) if x_first else (y, x)

        def slot(i1, i2):
            return i2 * RX + i1 if x_first else i1 * RX + i2

        def send(n, src, axis, step):
            i1, i2 = me1, me2
            if axis == 1:
                i1 = (me1 + step) % 4
            else:
                i2 = (me2 + step) % 4
            remote(
                buf.at[src], buf.at[src], g_send.at[c, n], g_recv.at[c, src],
                at_plane(slot(i1, i2)),
            ).start()

        def recv(src):
            remote(
                buf.at[src], buf.at[src], g_send.at[c, 0], g_recv.at[c, src],
                at_plane(p),
            ).wait_recv()

        def src(o1, o2):
            return slot((me1 + o1 + 4) % 4, (me2 + o2 + 4) % 4)

        return send, recv, src, forward

    rings = [
        make_ring(0, t0, True, 1), make_ring(1, s0, True, -1),
        make_ring(2, t1, False, 1), make_ring(3, s1, False, -1),
    ]
    for send, recv, src, f in rings:
        send(0, src(0, 0), 1, 1)
        send(1, src(0, 0), 1, -1)
    for send, recv, src, f in rings:
        send(2, src(0, 0), 2, 1)
        send(3, src(0, 0), 2, -1)
    for send, recv, src, f in rings:
        recv(src(-f, 0))
        send(4, src(-f, 0), 1, f)
        send(5, src(-f, 0), 2, 1)
        send(6, src(-f, 0), 2, -1)
        recv(src(f, 0))
        send(7, src(f, 0), 2, 1)
        send(8, src(f, 0), 2, -1)
    for send, recv, src, f in rings:
        recv(src(0, -f))
        send(9, src(0, -f), 2, f)
    for send, recv, src, f in rings:
        recv(src(2, 0))
        send(10, src(2, 0), 2, 1)
        send(11, src(2, 0), 2, -1)
    for n, o in ((12, -1), (13, 1), (14, 2)):
        for send, recv, src, f in rings:
            recv(src(o, -f))
            send(n, src(o, -f), 2, f)
    for o in (0, -1, 1, 2):
        for send, recv, src, f in rings:
            recv(src(o, f))
            recv(src(o, 2))

    for copy in l_copies:
        copy.wait()
    for copy in w_copies:
        copy.wait()

    def rows_of(buf):
        return buf[...].astype(F32).reshape(PLANE * 8, buf.shape[2]).astype(BF16)

    xt[:, : dt // 2] = rows_of(t0)
    xt[:, dt // 2 :] = rows_of(t1)
    xs[:, : ds // 2] = rows_of(s0)
    xs[:, ds // 2 :] = rows_of(s1)
    sums = [jnp.zeros((1, 128), F32) for _ in range(7)]
    for half in range(2):
        raw_t[...] = lax.dot_general(wt[half], xt[...], NT, preferred_element_type=F32)
        raw_s[...] = lax.dot_general(ws[half], xs[...], NT, preferred_element_type=F32)
        vocab0 = ((p * 2 + half) * RZ + z) * vloc
        ids = vocab0 + lax.broadcasted_iota(jnp.int32, (vloc, 128), 0)
        onehot = ids == labels
        rs = raw_s[...]
        tan_t = jnp.tanh(raw_t[...] * (1.0 / CAP))
        tan_s = jnp.tanh(rs * (1.0 / CAP))
        log_t = CAP * tan_t
        log_s = CAP * tan_s
        exp_t = jnp.exp(log_t)
        exp_s = jnp.exp(log_s)
        slope = 1.0 - tan_s * tan_s
        e_s = exp_s * slope
        e_t = exp_t * slope
        o_h = jnp.where(onehot, slope, 0.0)
        es_s[half] = e_s
        et_s[half] = e_t
        oh_s[half] = o_h
        terms = (
            exp_t, exp_s, exp_t * (log_t - log_s), jnp.where(onehot, log_s, 0.0),
            e_s * rs, e_t * rs, o_h * rs,
        )
        sums = [a + jnp.sum(v, axis=0, keepdims=True) for a, v in zip(sums, terms)]

    sxy[p] = jnp.concatenate(sums + [jnp.zeros((1, 128), F32)], axis=0)

    def a_copy(k, slot):
        return remote(
            sxy.at[p], sxy.at[slot], a_send.at[k], a_recv.at[slot],
            at_plane((p + k) % PLANE),
        )

    def b_copy(k, slot):
        return remote(
            sz.at[z], sz.at[slot], b_send.at[k], b_recv.at[slot],
            at_line((z + k) % RZ),
        )

    @pl.loop(1, PLANE)
    def _(k):
        a_copy(k, p).start()

    @pl.loop(1, PLANE)
    def _(k):
        a_copy(k, (p + k) % PLANE).wait_recv()

    sz[z] = jnp.sum(sxy[...], axis=0)

    @pl.loop(1, RZ)
    def _(k):
        b_copy(k, z).start()

    @pl.loop(1, RZ)
    def _(k):
        b_copy(k, (z + k) % RZ).wait_recv()

    total = jnp.sum(sz[...], axis=0)
    sum_t, sum_s, cross, picked = (total[i : i + 1] for i in range(4))
    scale_s = 2.0 / sum_s
    scale_t = 1.0 / sum_t

    for half in range(2):
        grad = es_s[half] * scale_s - et_s[half] * scale_t - oh_s[half]
        gbuf[:, half * vloc : (half + 1) * vloc] = grad.T.astype(BF16)
    part = 512
    for n in range(ds // part):
        cut = slice(n * part, (n + 1) * part)
        term = jnp.dot(
            gbuf[:, :vloc], ws[0, :, cut], preferred_element_type=F32
        ) + jnp.dot(gbuf[:, vloc:], ws[1, :, cut], preferred_element_type=F32)
        obuf[:, :, cut] = term.reshape(PLANE, 8, part).astype(BF16)

    def r_copy(k, src, slot):
        return remote(
            obuf.at[src], rbuf.at[slot], r_send.at[k], r_recv.at[slot],
            at_plane((p + k) % PLANE),
        )

    @pl.loop(1, PLANE)
    def _(k):
        r_copy(k, (p + k) % PLANE, p).start()

    loss = cross / sum_t - jnp.log(sum_t) + 2.0 * jnp.log(sum_s) - picked
    radial = scale_s * total[4:5] - scale_t * total[5:6] - total[6:7]
    packed = jnp.concatenate([loss, radial, jnp.zeros((6, 128), F32)], axis=0)
    cols[...] = packed.T
    mine = cols[pl.ds(p * 8, 8), :]
    loss_ref[...] = mine[:, :1]
    rad = mine[:, 1:2]

    rbuf[p] = obuf[p]

    @pl.loop(1, PLANE)
    def _(k):
        r_copy(k, (p + k) % PLANE, (p + k) % PLANE).wait_recv()

    back = jnp.sum(rbuf[...].astype(F32), axis=0) * gain_s
    for k in range(RZ):
        zsend[k, :, :sl] = back[:, k * sl : (k + 1) * sl].astype(BF16)

    def q_copy(k, src, slot):
        return remote(
            zsend.at[src], zrecv.at[slot], q_send.at[k], q_recv.at[slot],
            at_line((z + k) % RZ),
        )

    @pl.loop(1, RZ)
    def _(k):
        q_copy(k, (z + k) % RZ, z).start()

    zrecv[z] = zsend[z]

    @pl.loop(1, RZ)
    def _(k):
        q_copy(k, (z + k) % RZ, (z + k) % RZ).wait_recv()

    sum_back = jnp.sum(zrecv[...].astype(F32), axis=0)[:, :sl]
    out = inv_s * sum_back - (inv_s * inv_s * rad) * sh_ref[...].astype(F32) / ds
    grad_ref[...] = out.astype(BF16)

    @pl.loop(1, RZ)
    def _(k):
        z_copy(k, z).wait_send()
        a_copy(k, p).wait_send()
        b_copy(k, z).wait_send()
        r_copy(k, p, p).wait_send()
        q_copy(k, z, z).wait_send()

    for c, buf in enumerate((t0, s0, t1, s1)):
        @pl.loop(0, 15)
        def _(n):
            remote(
                buf.at[p], buf.at[p], g_send.at[c, n], g_recv.at[c, p], at_plane(p)
            ).wait_send()


def on_device(th, sh, tg, sg, wt, ws, labels):
    tok, tl = th.shape
    sl = sh.shape[1]
    dt, ds, vloc = tl * RZ, sl * RZ, wt.shape[0]
    vmem = pl.BlockSpec(memory_space=pltpu.VMEM)
    hbm = pl.BlockSpec(memory_space=pl.ANY)
    dma = pltpu.SemaphoreType.DMA
    grad, loss = pl.pallas_call(
        kernel,
        out_shape=(
            jax.ShapeDtypeStruct((tok, sl), BF16),
            jax.ShapeDtypeStruct((tok, 1), F32),
        ),
        in_specs=[vmem] * 5 + [hbm] * 2,
        out_specs=(vmem, vmem),
        scratch_shapes=[
            pltpu.VMEM((2, vloc, dt), BF16),
            pltpu.VMEM((2, vloc, ds), BF16),
            pltpu.VMEM((RZ, tok, tl + sl), BF16),
            pltpu.VMEM((PLANE, tok, dt // 2), BF16),
            pltpu.VMEM((PLANE, tok, dt // 2), BF16),
            pltpu.VMEM((PLANE, tok, ds // 2), BF16),
            pltpu.VMEM((PLANE, tok, ds // 2), BF16),
            pltpu.VMEM((128, dt), BF16),
            pltpu.VMEM((128, ds), BF16),
            pltpu.VMEM((vloc, 128), F32),
            pltpu.VMEM((vloc, 128), F32),
            pltpu.VMEM((2, vloc, 128), F32),
            pltpu.VMEM((2, vloc, 128), F32),
            pltpu.VMEM((2, vloc, 128), F32),
            pltpu.VMEM((PLANE, 8, 128), F32),
            pltpu.VMEM((RZ, 8, 128), F32),
            pltpu.VMEM((128, 2 * vloc), BF16),
            pltpu.VMEM((PLANE, tok, ds), BF16),
            pltpu.VMEM((PLANE, tok, ds), BF16),
            pltpu.VMEM((RZ, tok, 256), BF16),
            pltpu.VMEM((RZ, tok, 256), BF16),
            pltpu.VMEM((128, 8), F32),
            dma((2,)), dma((2,)), dma((2,)),
            dma((RZ,)), dma((RZ,)),
            dma((4, 15)), dma((4, PLANE)),
            dma((PLANE,)), dma((PLANE,)),
            dma((RZ,)), dma((RZ,)),
            dma((PLANE,)), dma((PLANE,)),
            dma((RZ,)), dma((RZ,)),
        ],
        compiler_params=pltpu.CompilerParams(
            collective_id=0, has_side_effects=True, vmem_limit_bytes=56 * 1024 * 1024
        ),
    )(th, sh, tg.reshape(1, dt), sg.reshape(1, ds), labels.reshape(2, 128), wt, ws)
    return (loss.reshape(tok), grad)


def solution(mesh):
    in_specs = (
        P("dp", ("group", "tensor")),
        P("dp", ("group", "tensor")),
        P(),
        P(),
        P(("dp", "group", "tensor"), None),
        P(("dp", "group", "tensor"), None),
        P(),
    )
    out_specs = (P("dp"), P("dp", ("group", "tensor")))
    return jax.shard_map(
        on_device, mesh=mesh, in_specs=in_specs, out_specs=out_specs, check_vma=False
    )
```

time: 451 us -> 84.2 us (0.19)
  the two profiles are of different devices: /device:TPU:32 before, /device:TPU:8 now
where the time goes in v1:
time: 84.2 us; the launch traced here: 83.8 us
  Pallas kernels  78 us (93%)
  local copies, waits for them, and re-layouts  3.88 us (5%)
  other arithmetic  1.3 us (2%)
    pallas_call x1, Pallas kernels, on_device(): pl.pallas_call(kernel, out_shape=(jax.ShapeDtypeStruct((tok, sl), BF16),...  78 us

profile of v1, /device:TPU:8, one launch (start us, length us, event | category | flops | bytes accessed | tf_op | source)
XLA Modules:
  0.0 83.8 jit_solution(14639123262983362024)
XLA Ops:
  0.6 1.3 %reshape.17.sg_ref = bf16[1,3584]{1,0:T(2,128)(2,1)} reshape(bf16[3584]{0:T(1024)(128)(2,1)} %param.10) | data formatting | bytes 14336 | tf_op jit(solution)/shard_map/reshape | solution.py:382
  1.9 1.3 %reshape.16.tg_ref = bf16[1,4608]{1,0:T(2,128)(2,1)} reshape(bf16[4608]{0:T(1024)(128)(2,1)} %param.9) | data formatting | bytes 18432 | tf_op jit(solution)/shard_map/reshape | solution.py:382
  3.2 78.0 %shard_map.86 = (bf16[8,224]{1,0:T(8,128)(2,1)}, f32[8,1]{1,0:T(8,128)}) custom-call(bf16[8,288]{1,0:T(8,128)(2,1)} %th_ref.1, bf16[8,224]{1,0:T(8,128)(2,1)} %sh_ref.1, bf16[1,4608]{1,0:T(2,128)(2,1)} %reshape.16.tg_ref, bf16[1,3584]{1,0:T(2,128)(2,1)} %reshape.17.sg_ref, s32[2,128]{1,0:T(2,128)} %bitcast.1, bf16[256,4608]{1,0:T(8,128)(2,1)} %wt_hbm.1, ...), custom_call_target="tpu_custom_call" | custom-call | tf_op jit(solution)/shard_map/pallas_call | solution.py:340
  81.2 1.3 %reduce = f32[8]{0:T(128)} reduce(f32[8,1]{1,0:T(8,128)} %get-tuple-element.4, f32[]{:T(128)} %constant.4), dimensions={1}, to_apply=%get-tuple-element.4.reduce_sub_computation | reduce | bytes 68 | tf_op jit(solution)/shard_map/pallas_call | solution.py:340
  82.5 1.3 %copy.10 = bf16[8,224]{1,0:T(8,128)(2,1)} copy(bf16[8,224]{1,0:T(8,128)(2,1)} %get-tuple-element.9) | data formatting | bytes 7168

commit v2 on v1

v2 whole, which is shorter than its diff:
```python
import jax
import jax.numpy as jnp
from jax import lax
from jax.experimental import pallas as pl
from jax.experimental.pallas import tpu as pltpu
from jax.sharding import PartitionSpec as P

CAP = 30.0
EPS = 1e-06
MESH = pl.DeviceIdType.MESH
F32 = jnp.float32
BF16 = jnp.bfloat16
RX, RY, RZ = 4, 4, 16
PLANE = RX * RY
NT = (((1,), (1,)), ((), ()))


def kernel(
    th_ref, sh_ref, tg_ref, sg_ref, lab_ref, wt_hbm, ws_hbm,
    out_ref,
    wt, ws, buf, ibuf, gt, gs, raw_t, raw_s, es_s, et_s, oh_s,
    sxy, sz, gbuf, obuf, rbuf, zsend, zrecv, cols,
    w_send, w_recv, w_loc, z_send, z_recv, g_send, g_recv, i_send, i_recv,
    a_send, a_recv, b_send, b_recv, r_send, r_recv, q_send, q_recv,
):
    dp = lax.axis_index("dp")
    z = lax.axis_index("group") * 8 + lax.axis_index("tensor")
    core = dp % 2
    p = dp // 2
    x = p % RX
    y = p // RX
    quad = z // 4
    tl = th_ref.shape[1]
    sl = sh_ref.shape[1]
    ds = sl * RZ
    vloc = wt_hbm.shape[0]

    def at_plane(q):
        return (q * 2 + core, lax.axis_index("group"), lax.axis_index("tensor"))

    def at_line(k):
        return (dp, k // 8, k % 8)

    partner = (p * 2 + 1 - core, lax.axis_index("group"), lax.axis_index("tensor"))

    def remote(src, dst, send, recv, device):
        return pltpu.make_async_remote_copy(
            src_ref=src, dst_ref=dst, send_sem=send, recv_sem=recv,
            device_id=device, device_id_type=MESH,
        )

    barrier = pltpu.get_barrier_semaphore()

    @pl.loop(1, RZ)
    def _(k):
        pl.semaphore_signal(
            barrier, inc=1, device_id=at_line((z + k) % RZ), device_id_type=MESH
        )
        pl.semaphore_signal(
            barrier, inc=1, device_id=at_plane((p + k) % PLANE), device_id_type=MESH
        )

    pl.semaphore_signal(barrier, inc=1, device_id=partner, device_id_type=MESH)

    l_copies = [
        pltpu.make_async_copy(wt_hbm, wt.at[core], w_loc.at[0]),
        pltpu.make_async_copy(ws_hbm, ws.at[core], w_loc.at[1]),
    ]
    for copy in l_copies:
        copy.start()

    own = jnp.concatenate(
        [th_ref[...].astype(F32), sh_ref[...].astype(F32)], axis=1
    )
    buf[quad, p, z % 4] = own.astype(BF16)

    for gain_ref, wide in ((tg_ref, gt), (sg_ref, gs)):
        gain = gain_ref[...].astype(F32)
        for i in range(gain.shape[0]):
            wide[:, i * 128 : (i + 1) * 128] = gain[i : i + 1]

    lane = lax.broadcasted_iota(jnp.int32, (8, 128), 1)
    label_row = jnp.zeros((8, 128), jnp.int32)
    for q in range(PLANE):
        row = jnp.broadcast_to(lab_ref[q // 8 : q // 8 + 1, :], (8, 128))
        shift = (8 * q - 16 * (q % 8) - 8 * core + 256) % 128
        label_row = jnp.where(lane // 8 == q, pltpu.roll(row, shift, 1), label_row)
    labels = label_row[:1, :]

    pl.semaphore_wait(barrier, 31)

    def await_recv(ref, sem):
        remote(ref, ref, w_send.at[0], sem, partner).wait_recv()

    def await_send(ref, sem):
        remote(ref, ref, sem, w_recv.at[0], partner).wait_send()

    slab = buf.at[quad, p, z % 4]

    def z_start(k):
        to = (z + k + RZ) % RZ
        remote(
            slab, slab, z_send.at[0], z_recv.at[(quad - to // 4 + 4) % 4], at_line(to)
        ).start()

    @pl.loop(1, 8)
    def _(k):
        z_start(k)
        z_start(-k)

    z_start(8)

    w_copies = [
        remote(wt_hbm, wt.at[core], w_send.at[0], w_recv.at[0], partner),
        remote(ws_hbm, ws.at[core], w_send.at[1], w_recv.at[1], partner),
    ]
    for copy in w_copies:
        copy.start()

    class Ring:
        def __init__(self, c, delta, x_first):
            self.c, self.q, self.delta = c, (quad + delta) % 4, delta
            self.x_first = x_first
            self.me1, self.me2 = (x, y) if x_first else (y, x)

        def src(self, o1, o2):
            i1, i2 = (self.me1 + o1 + 4) % 4, (self.me2 + o2 + 4) % 4
            return i2 * RX + i1 if self.x_first else i1 * RX + i2

        def send(self, o1, to1, to2, sem):
            ref = buf.at[self.q, self.src(o1, 0)]
            remote(
                ref, ref, g_send.at[self.c], g_recv.at[self.c, sem],
                at_plane(self.src(to1, to2)),
            ).start()

        def begin(self):
            n = 3 if self.delta == 0 else 4
            await_recv(buf.at[self.q, p, pl.ds(0, n)], z_recv.at[self.delta])
            for o in (1, -1, 2):
                self.send(0, o, 0, o + 1)
            for o in (1, -1, 2):
                self.send(0, 0, o, 1)

        def middle(self):
            for o in (-1, 1, 2):
                await_recv(buf.at[self.q, p], g_recv.at[self.c, {-1: 2, 1: 0, 2: 3}[o]])
                for to in (1, -1, 2):
                    self.send(o, 0, to, 1)

        def finish(self):
            await_recv(buf.at[self.q, pl.ds(0, 12)], g_recv.at[self.c, 1])

    r0, r1, r2, r3 = rings = [
        Ring(0, 0, True), Ring(1, 1, False), Ring(2, 3, True), Ring(3, 2, False)
    ]
    r0.begin()
    r1.begin()
    r2.begin()
    r0.middle()
    r3.begin()
    squares = jnp.zeros((8, tl + sl), F32)
    for k in range(4):
        for j in range(4):
            v = buf[k, p, j].astype(F32)
            squares = squares + v * v
    own_t = jnp.sum(squares[:, :tl], axis=1, keepdims=True)
    own_s = jnp.sum(squares[:, tl:], axis=1, keepdims=True)
    inv_t = lax.rsqrt(own_t / (tl * RZ) + EPS)
    inv_s = lax.rsqrt(own_s / ds + EPS)
    ibuf[p] = jnp.where(lane == 0, inv_t, inv_s)

    def i_copy(k):
        return remote(
            ibuf.at[p], ibuf.at[p], i_send.at[0], i_recv.at[0],
            at_plane((p + k) % PLANE),
        )

    @pl.loop(1, PLANE)
    def _(k):
        i_copy(k).start()

    r1.middle()
    r2.middle()
    r3.middle()
    await_recv(ibuf.at[pl.ds(0, PLANE - 1)], i_recv.at[0])
    for copy in l_copies:
        copy.wait()
    for copy in w_copies:
        copy.wait()

    all_t = ibuf[:, :, 0:1].reshape(PLANE * 8, 1)
    all_s = ibuf[:, :, 1:2].reshape(PLANE * 8, 1)

    def multiply(ring):
        pieces = [
            buf[ring.q, :, j].astype(F32).reshape(PLANE * 8, tl + sl) for j in range(4)
        ]
        cut_t = pl.ds(pl.multiple_of(ring.q * (4 * tl), 128), 4 * tl)
        cut_s = pl.ds(pl.multiple_of(ring.q * (4 * sl), 128), 4 * sl)
        v_t = jnp.concatenate([v[:, :tl] for v in pieces], axis=1)
        v_s = jnp.concatenate([v[:, tl:] for v in pieces], axis=1)
        x_t = (v_t * all_t * gt[:, cut_t]).astype(BF16)
        x_s = (v_s * all_s * gs[:, cut_s]).astype(BF16)
        for half in range(2):
            d_t = lax.dot_general(wt[half, :, cut_t], x_t, NT, preferred_element_type=F32)
            d_s = lax.dot_general(ws[half, :, cut_s], x_s, NT, preferred_element_type=F32)
            if ring.c == 0:
                raw_t[half] = d_t
                raw_s[half] = d_s
            else:
                raw_t[half] += d_t
                raw_s[half] += d_s

    r0.finish()
    multiply(r0)
    r1.finish()
    multiply(r1)
    r2.finish()
    multiply(r2)
    r3.finish()
    multiply(r3)

    sums = [jnp.zeros((1, 128), F32) for _ in range(7)]
    for half in range(2):
        vocab0 = ((p * 2 + half) * RZ + z) * vloc
        ids = vocab0 + lax.broadcasted_iota(jnp.int32, (vloc, 128), 0)
        onehot = ids == labels
        rs = raw_s[half]
        tan_t = jnp.tanh(raw_t[half] * (1.0 / CAP))
        tan_s = jnp.tanh(rs * (1.0 / CAP))
        log_t = CAP * tan_t
        log_s = CAP * tan_s
        exp_t = jnp.exp(log_t)
        exp_s = jnp.exp(log_s)
        slope = 1.0 - tan_s * tan_s
        e_s = exp_s * slope
        e_t = exp_t * slope
        o_h = jnp.where(onehot, slope, 0.0)
        es_s[half] = e_s
        et_s[half] = e_t
        oh_s[half] = o_h
        terms = (
            exp_t, exp_s, exp_t * (log_t - log_s), jnp.where(onehot, log_s, 0.0),
            e_s * rs, e_t * rs, o_h * rs,
        )
        sums = [a + jnp.sum(v, axis=0, keepdims=True) for a, v in zip(sums, terms)]

    sxy[p] = jnp.concatenate(sums + [jnp.zeros((1, 128), F32)], axis=0)

    def a_copy(k):
        return remote(
            sxy.at[p], sxy.at[p], a_send.at[0], a_recv.at[0],
            at_plane((p + k) % PLANE),
        )

    def b_copy(k):
        return remote(
            sz.at[z], sz.at[z], b_send.at[0], b_recv.at[0],
            at_line((z + k) % RZ),
        )

    @pl.loop(1, PLANE)
    def _(k):
        a_copy(k).start()

    await_recv(sxy.at[pl.ds(0, PLANE - 1)], a_recv.at[0])

    sz[z] = jnp.sum(sxy[...], axis=0)

    @pl.loop(1, RZ)
    def _(k):
        b_copy(k).start()

    await_recv(sz.at[pl.ds(0, RZ - 1)], b_recv.at[0])

    total = jnp.sum(sz[...], axis=0)
    sum_t, sum_s, cross, picked = (total[i : i + 1] for i in range(4))
    scale_s = 2.0 / sum_s
    scale_t = 1.0 / sum_t

    for half in range(2):
        grad = es_s[half] * scale_s - et_s[half] * scale_t - oh_s[half]
        gbuf[:, half * vloc : (half + 1) * vloc] = grad.T.astype(BF16)
    part = 512
    for n in range(ds // part):
        cut = slice(n * part, (n + 1) * part)
        term = jnp.dot(
            gbuf[:, :vloc], ws[0, :, cut], preferred_element_type=F32
        ) + jnp.dot(gbuf[:, vloc:], ws[1, :, cut], preferred_element_type=F32)
        obuf[:, :, cut] = term.reshape(PLANE, 8, part).astype(BF16)

    def r_copy(k):
        to = (p + k) % PLANE
        return remote(
            obuf.at[to], rbuf.at[p], r_send.at[0], r_recv.at[0], at_plane(to)
        )

    @pl.loop(1, PLANE)
    def _(k):
        r_copy(k).start()

    loss = cross / sum_t - jnp.log(sum_t) + 2.0 * jnp.log(sum_s) - picked
    radial = scale_s * total[4:5] - scale_t * total[5:6] - total[6:7]
    packed = jnp.concatenate([loss, radial, jnp.zeros((6, 128), F32)], axis=0)
    cols[...] = packed.T
    mine = cols[pl.ds(p * 8, 8), :]
    out_ref[:, 256:] = jnp.broadcast_to(mine[:, :1], (8, 128))
    rad = mine[:, 1:2]

    rbuf[p] = obuf[p]

    await_recv(rbuf.at[pl.ds(0, PLANE - 1)], r_recv.at[0])

    back = jnp.sum(rbuf[...].astype(F32), axis=0) * gs[...]
    for k in range(RZ):
        zsend[k, :, :sl] = back[:, k * sl : (k + 1) * sl].astype(BF16)

    def q_copy(k):
        to = (z + k) % RZ
        return remote(
            zsend.at[to], zrecv.at[z], q_send.at[0], q_recv.at[0], at_line(to)
        )

    @pl.loop(1, RZ)
    def _(k):
        q_copy(k).start()

    await_send(buf.at[0, pl.ds(0, RZ - 1), 0], z_send.at[0])
    await_send(ibuf.at[pl.ds(0, PLANE - 1)], i_send.at[0])
    await_send(sxy.at[pl.ds(0, PLANE - 1)], a_send.at[0])
    await_send(sz.at[pl.ds(0, RZ - 1)], b_send.at[0])
    for ring in rings:
        await_send(buf.at[ring.q, pl.ds(0, 15)], g_send.at[ring.c])

    zrecv[z] = zsend[z]

    await_recv(zrecv.at[pl.ds(0, RZ - 1)], q_recv.at[0])

    sum_back = jnp.sum(zrecv[...].astype(F32), axis=0)[:, :sl]
    out = inv_s * sum_back - (inv_s * inv_s * rad) * sh_ref[...].astype(F32) / ds
    out_ref[:, :sl] = out

    await_send(obuf.at[pl.ds(0, PLANE - 1)], r_send.at[0])
    await_send(zsend.at[pl.ds(0, RZ - 1)], q_send.at[0])


def on_device(th, sh, tg, sg, wt, ws, labels):
    tok, tl = th.shape
    sl = sh.shape[1]
    dt, ds, vloc = tl * RZ, sl * RZ, wt.shape[0]
    vmem = pl.BlockSpec(memory_space=pltpu.VMEM)
    hbm = pl.BlockSpec(memory_space=pl.ANY)
    dma = pltpu.SemaphoreType.DMA
    out = pl.pallas_call(
        kernel,
        out_shape=jax.ShapeDtypeStruct((tok, 384), F32),
        in_specs=[vmem] * 5 + [hbm] * 2,
        out_specs=vmem,
        scratch_shapes=[
            pltpu.VMEM((2, vloc, dt), BF16),
            pltpu.VMEM((2, vloc, ds), BF16),
            pltpu.VMEM((4, PLANE, 4, tok, tl + sl), BF16),
            pltpu.VMEM((PLANE, tok, 128), F32),
            pltpu.VMEM((1, dt), F32),
            pltpu.VMEM((1, ds), F32),
            pltpu.VMEM((2, vloc, 128), F32),
            pltpu.VMEM((2, vloc, 128), F32),
            pltpu.VMEM((2, vloc, 128), F32),
            pltpu.VMEM((2, vloc, 128), F32),
            pltpu.VMEM((2, vloc, 128), F32),
            pltpu.VMEM((PLANE, 8, 128), F32),
            pltpu.VMEM((RZ, 8, 128), F32),
            pltpu.VMEM((128, 2 * vloc), BF16),
            pltpu.VMEM((PLANE, tok, ds), BF16),
            pltpu.VMEM((PLANE, tok, ds), BF16),
            pltpu.VMEM((RZ, tok, 256), BF16),
            pltpu.VMEM((RZ, tok, 256), BF16),
            pltpu.VMEM((128, 8), F32),
            dma((2,)), dma((2,)), dma((2,)),
            dma((1,)), dma((4,)),
            dma((4,)), dma((4, 4)),
            dma((1,)), dma((1,)),
            dma((1,)), dma((1,)),
            dma((1,)), dma((1,)),
            dma((1,)), dma((1,)),
            dma((1,)), dma((1,)),
        ],
        compiler_params=pltpu.CompilerParams(
            collective_id=0, has_side_effects=True, vmem_limit_bytes=56 * 1024 * 1024
        ),
    )(th, sh, tg.reshape(-1, 128), sg.reshape(-1, 128), labels.reshape(2, 128), wt, ws)
    return (out[:, 256], out[:, :sl].astype(BF16))


def solution(mesh):
    in_specs = (
        P("dp", ("group", "tensor")),
        P("dp", ("group", "tensor")),
        P(),
        P(),
        P(("dp", "group", "tensor"), None),
        P(("dp", "group", "tensor"), None),
        P(),
    )
    out_specs = (P("dp"), P("dp", ("group", "tensor")))
    return jax.shard_map(
        on_device, mesh=mesh, in_specs=in_specs, out_specs=out_specs, check_vma=False
    )
```

time: 84.2 us -> 77.9 us (0.925)
  Pallas kernels: 78 us -> 74.4 us
  other arithmetic: 1.3 us -> 0 us
  local copies, waits for them, and re-layouts: 3.88 us -> 2.59 us
    pallas_call x1, Pallas kernels: 78 us -> 74.4 us  [on_device(): pl.pallas_call(kernel, out_shape=jax.ShapeDtypeStruct((tok, 384), F32), i...]
    reshape x2 -> x0, local copies, waits for them, and re-layouts: 2.61 us -> none  [the longest x1 1.31 us: on_device(): tg.reshape(1, dt)]
    slice x0 -> x2, local copies, waits for them, and re-layouts: none -> 2.59 us  [on_device(): return (out[:, 256], out[:, :sl].astype(BF16))]
    pallas_call x1 -> x0, other arithmetic: 1.3 us -> none  [on_device(): pl.pallas_call(kernel, out_shape=(jax.ShapeDtypeStruct((tok, sl), BF16),...]
    unnamed x1 -> x0, local copies, waits for them, and re-layouts: 1.27 us -> none
where the time goes in v2:
time: 77.9 us; the launch traced here: 77.6 us
  Pallas kernels  74.4 us (96%)
  local copies, waits for them, and re-layouts  2.59 us (3%)
    pallas_call x1, Pallas kernels, on_device(): pl.pallas_call(kernel, out_shape=jax.ShapeDtypeStruct((tok, 384), F32), i...  74.4 us
    slice x2, local copies, waits for them, and re-layouts, on_device(): return (out[:, 256], out[:, :sl].astype(BF16))  2.59 us

profile of v2, /device:TPU:8, one launch (start us, length us, event | category | flops | bytes accessed | tf_op | source)
XLA Modules:
  0.0 77.6 jit_solution(14203407519526426966)
XLA Ops:
  0.6 74.4 %shard_map.86 = f32[8,384]{1,0:T(8,128)} custom-call(bf16[8,288]{1,0:T(8,128)(2,1)} %th_ref.1, bf16[8,224]{1,0:T(8,128)(2,1)} %sh_ref.1, bf16[36,128]{1,0:T(8,128)(2,1)} %bitcast.3, bf16[28,128]{1,0:T(8,128)(2,1)} %bitcast.4, s32[2,128]{1,0:T(2,128)} %bitcast.5, bf16[256,4608]{1,0:T(8,128)(2,1)} %wt_hbm.1, bf16[256,3584]{1,0:T(8,128)(2,1)} %ws_hbm.1), custom_call_target="tpu_custom_call" | custom-call | tf_op jit(solution)/shard_map/pallas_call | solution.py:355
  75.0 1.3 %slice_reduce_fusion = f32[8]{0:T(128)} fusion(f32[8,384]{1,0:T(8,128)} %shard_map.86), kind=kLoop, calls=%fused_computation.1 | loop fusion | bytes 64 | tf_op jit(solution)/shard_map/slice | solution.py:393
  76.3 1.3 %slice.12 = bf16[8,224]{1,0:T(8,128)(2,1)} slice(f32[8,384]{1,0:T(8,128)} %shard_map.86), slice={[0:8], [0:224]} | slice | bytes 7168 | tf_op jit(solution)/shard_map/slice | solution.py:393

commit v3 on v2

--- a/solution.py
+++ b/solution.py
@@ -16,11 +16,11 @@
 
 
 def kernel(
-    th_ref, sh_ref, tg_ref, sg_ref, lab_ref, wt_hbm, ws_hbm,
+    th_hbm, sh_hbm, tg_hbm, sg_hbm, lab_hbm, wt_hbm, ws_hbm,
     out_ref,
-    wt, ws, buf, ibuf, gt, gs, raw_t, raw_s, es_s, et_s, oh_s,
+    th_ref, sh_ref, tg_ref, sg_ref, lab_ref, wt, ws, buf, ibuf, gt, gs, raw_t, raw_s, es_s, et_s, oh_s,
     sxy, sz, gbuf, obuf, rbuf, zsend, zrecv, cols,
-    w_send, w_recv, w_loc, z_send, z_recv, g_send, g_recv, i_send, i_recv,
+    w_send, w_recv, w_loc, s_loc, z_send, z_recv, g_send, g_recv, i_send, i_recv,
     a_send, a_recv, b_send, b_recv, r_send, r_recv, q_send, q_recv,
 ):
     dp = lax.axis_index("dp")
@@ -49,6 +49,18 @@
             device_id=device, device_id_type=MESH,
         )
 
+    small = [
+        pltpu.make_async_copy(src, dst, s_loc.at[i])
+        for i, (src, dst) in enumerate(
+            (
+                (th_hbm, th_ref), (sh_hbm, sh_ref), (tg_hbm, tg_ref),
+                (sg_hbm, sg_ref), (lab_hbm, lab_ref),
+            )
+        )
+    ]
+    for copy in small:
+        copy.start()
+
     barrier = pltpu.get_barrier_semaphore()
 
     @pl.loop(1, RZ)
@@ -68,6 +80,9 @@
     ]
     for copy in l_copies:
         copy.start()
+
+    for copy in small:
+        copy.wait()
 
     own = jnp.concatenate(
         [th_ref[...].astype(F32), sh_ref[...].astype(F32)], axis=1
@@ -118,46 +133,109 @@
         copy.start()
 
     class Ring:
-        def __init__(self, c, delta, x_first):
+        def __init__(self, c, delta, x_first, way):
             self.c, self.q, self.delta = c, (quad + delta) % 4, delta
-            self.x_first = x_first
+            self.x_first, self.way = x_first, way
             self.me1, self.me2 = (x, y) if x_first else (y, x)
+            self.alone = {
+                ("first", 1): 0, ("first", -1): 1, ("far", 0): 2,
+                ("second", 0): 3, ("second", -1): 4, ("second", 1): 5, ("second", 2): 6,
+            }
 
         def src(self, o1, o2):
             i1, i2 = (self.me1 + o1 + 4) % 4, (self.me2 + o2 + 4) % 4
             return i2 * RX + i1 if self.x_first else i1 * RX + i2
 
-        def send(self, o1, to1, to2, sem):
-            ref = buf.at[self.q, self.src(o1, 0)]
+        def send(self, o1, o2, to1, to2, sem):
+            ref = buf.at[self.q, self.src(o1, o2)]
             remote(
                 ref, ref, g_send.at[self.c], g_recv.at[self.c, sem],
                 at_plane(self.src(to1, to2)),
             ).start()
 
+        def wait(self, sem):
+            await_recv(buf.at[self.q, p], g_recv.at[self.c, sem])
+
+        def second(self, o):
+            self.send(o, 0, 0, self.way, self.alone["second", o])
+            self.send(o, 0, 0, -self.way, 7)
+
         def begin(self):
-            n = 3 if self.delta == 0 else 4
+            n = 3 if self.c == 0 else 4
             await_recv(buf.at[self.q, p, pl.ds(0, n)], z_recv.at[self.delta])
-            for o in (1, -1, 2):
-                self.send(0, o, 0, o + 1)
-            for o in (1, -1, 2):
-                self.send(0, 0, o, 1)
+            for to in (1, -1):
+                self.send(0, 0, to, 0, self.alone["first", to])
+            self.second(0)
+
+        def near(self):
+            way = self.way
+            self.wait(self.alone["first", way])
+            self.send(-way, 0, way, 0, self.alone["far", 0])
+            self.second(-way)
+            self.wait(self.alone["first", -way])
+            self.second(way)
+
+        def far(self):
+            self.wait(self.alone["far", 0])
+            self.second(2)
+
+        def column(self, o):
+            self.wait(self.alone["second", o])
+            self.send(o, -self.way, 0, self.way, 7)
+
+        def finish(self):
+            await_recv(buf.at[self.q, pl.ds(0, 8)], g_recv.at[self.c, 7])
+
+    class TwoStep(Ring):
+        def begin(self):
+            await_recv(buf.at[self.q, p], z_recv.at[self.delta])
+            for sem, to in enumerate((1, -1, 2)):
+                self.send(0, 0, to, 0, sem)
+            for to in (1, -1, 2):
+                self.send(0, 0, 0, to, 7)
 
         def middle(self):
-            for o in (-1, 1, 2):
-                await_recv(buf.at[self.q, p], g_recv.at[self.c, {-1: 2, 1: 0, 2: 3}[o]])
+            for sem, o in enumerate((-1, 1, 2)):
+                self.wait(sem)
                 for to in (1, -1, 2):
-                    self.send(o, 0, to, 1)
+                    self.send(o, 0, 0, to, 7)
 
         def finish(self):
-            await_recv(buf.at[self.q, pl.ds(0, 12)], g_recv.at[self.c, 1])
-
+            await_recv(buf.at[self.q, pl.ds(0, 12)], g_recv.at[self.c, 7])
+
+
+    class TwoStep(Ring):
+        def begin(self):
+            await_recv(buf.at[self.q, p], z_recv.at[self.delta])
+            for sem, to in enumerate((1, -1, 2)):
+                self.send(0, 0, to, 0, sem)
+            for to in (1, -1, 2):
+                self.send(0, 0, 0, to, 7)
+
+        def middle(self):
+            for sem, o in enumerate((-1, 1, 2)):
+                self.wait(sem)
+                for to in (1, -1, 2):
+                    self.send(o, 0, 0, to, 7)
+
+        def finish(self):
+            await_recv(buf.at[self.q, pl.ds(0, 12)], g_recv.at[self.c, 7])
+
+    beside = jnp.where(z % 4 < 2, 3, 1)
     r0, r1, r2, r3 = rings = [
-        Ring(0, 0, True), Ring(1, 1, False), Ring(2, 3, True), Ring(3, 2, False)
+        Ring(0, 0, True, 1), Ring(1, beside, False, 1),
+        Ring(2, 4 - beside, True, -1), TwoStep(3, 2, False, -1),
     ]
     r0.begin()
     r1.begin()
+    r0.near()
+    r0.column(0)
     r2.begin()
-    r0.middle()
+    r1.near()
+    r1.column(0)
+    r0.far()
+    r0.column(-1)
+    r0.column(1)
     r3.begin()
     squares = jnp.zeros((8, tl + sl), F32)
     for k in range(4):
@@ -180,9 +258,17 @@
     def _(k):
         i_copy(k).start()
 
-    r1.middle()
-    r2.middle()
+    r2.near()
+    r2.column(0)
+    r1.far()
+    r1.column(-1)
+    r1.column(1)
+    r0.column(2)
     r3.middle()
+    r2.far()
+    r2.column(-1)
+    r2.column(1)
+    r1.column(2)
     await_recv(ibuf.at[pl.ds(0, PLANE - 1)], i_recv.at[0])
     for copy in l_copies:
         copy.wait()
@@ -214,6 +300,7 @@
 
     r0.finish()
     multiply(r0)
+    r2.column(2)
     r1.finish()
     multiply(r1)
     r2.finish()
@@ -305,7 +392,7 @@
     packed = jnp.concatenate([loss, radial, jnp.zeros((6, 128), F32)], axis=0)
     cols[...] = packed.T
     mine = cols[pl.ds(p * 8, 8), :]
-    out_ref[:, 256:] = jnp.broadcast_to(mine[:, :1], (8, 128))
+    out_ref[:, 256:] = pltpu.roll(packed, (128 - p * 8) % 128, 1)
     rad = mine[:, 1:2]
 
     rbuf[p] = obuf[p]
@@ -343,6 +430,11 @@
 
     await_send(obuf.at[pl.ds(0, PLANE - 1)], r_send.at[0])
     await_send(zsend.at[pl.ds(0, RZ - 1)], q_send.at[0])
+
+
+def unpack(out_ref, loss_ref, grad_ref):
+    loss_ref[...] = out_ref[0, 256 : 256 + loss_ref.shape[0]]
+    grad_ref[...] = out_ref[:, : grad_ref.shape[1]].astype(BF16)
 
 
 def on_device(th, sh, tg, sg, wt, ws, labels):
@@ -355,9 +447,14 @@
     out = pl.pallas_call(
         kernel,
         out_shape=jax.ShapeDtypeStruct((tok, 384), F32),
-        in_specs=[vmem] * 5 + [hbm] * 2,
+        in_specs=[hbm] * 7,
         out_specs=vmem,
         scratch_shapes=[
+            pltpu.VMEM((tok, tl), BF16),
+            pltpu.VMEM((tok, sl), BF16),
+            pltpu.VMEM((dt // 128, 128), BF16),
+            pltpu.VMEM((ds // 128, 128), BF16),
+            pltpu.VMEM((2, 128), jnp.int32),
             pltpu.VMEM((2, vloc, dt), BF16),
             pltpu.VMEM((2, vloc, ds), BF16),
             pltpu.VMEM((4, PLANE, 4, tok, tl + sl), BF16),
@@ -377,9 +474,9 @@
             pltpu.VMEM((RZ, tok, 256), BF16),
             pltpu.VMEM((RZ, tok, 256), BF16),
             pltpu.VMEM((128, 8), F32),
-            dma((2,)), dma((2,)), dma((2,)),
+            dma((2,)), dma((2,)), dma((2,)), dma((5,)),
             dma((1,)), dma((4,)),
-            dma((4,)), dma((4, 4)),
+            dma((4,)), dma((4, 8)),
             dma((1,)), dma((1,)),
             dma((1,)), dma((1,)),
             dma((1,)), dma((1,)),
@@ -390,7 +487,14 @@
             collective_id=0, has_side_effects=True, vmem_limit_bytes=56 * 1024 * 1024
         ),
     )(th, sh, tg.reshape(-1, 128), sg.reshape(-1, 128), labels.reshape(2, 128), wt, ws)
-    return (out[:, 256], out[:, :sl].astype(BF16))
+    return pl.pallas_call(
+        unpack,
+        out_shape=(
+            jax.ShapeDtypeStruct((tok,), F32), jax.ShapeDtypeStruct((tok, sl), BF16)
+        ),
+        in_specs=[vmem],
+        out_specs=(vmem, vmem),
+    )(out)
 
 
 def solution(mesh):

time: 77.9 us -> 75.8 us (0.973)
  the two profiles are of different devices: /device:TPU:8 before, /device:TPU:32 now
where the time goes in v3:
time: 75.8 us; the launch traced here: 75.5 us
  Pallas kernels  74.9 us (99%)
    pallas_call x1, Pallas kernels, on_device(): pl.pallas_call(kernel, out_shape=jax.ShapeDtypeStruct((tok, 384), F32), i...  73.6 us

profile of v3, /device:TPU:32, one launch (start us, length us, event | category | flops | bytes accessed | tf_op | source)
XLA Modules:
  0.0 75.5 jit_solution(8859111766124129760)
XLA Ops:
  0.6 73.6 %shard_map.86.out_ref = f32[8,384]{1,0:T(8,128)} custom-call(bf16[8,288]{1,0:T(8,128)(2,1)} %th_hbm.1, bf16[8,224]{1,0:T(8,128)(2,1)} %sh_hbm.1, bf16[36,128]{1,0:T(8,128)(2,1)} %bitcast.3, bf16[28,128]{1,0:T(8,128)(2,1)} %bitcast.4, s32[2,128]{1,0:T(2,128)} %bitcast.5, bf16[256,4608]{1,0:T(8,128)(2,1)} %wt_hbm.1, bf16[256,3584]{1,0:T(8,128)(2,1)} %ws_hbm.1), custom_call_target="tpu_custom_call" | custom-call | tf_op jit(solution)/shard_map/pallas_call | solution.py:447
  74.2 1.3 %shard_map.87 = (f32[8]{0:T(128)}, bf16[8,224]{1,0:T(8,128)(2,1)}) custom-call(f32[8,384]{1,0:T(8,128)} %shard_map.86.out_ref), custom_call_target="tpu_custom_call" | custom-call | tf_op jit(solution)/shard_map/pallas_call | solution.py:490

commit v4 on v3

--- a/solution.py
+++ b/solution.py
@@ -41,6 +41,7 @@
     def at_line(k):
         return (dp, k // 8, k % 8)
 
+    my_rows = pl.ds(pl.multiple_of(core * vloc, vloc), vloc)
     partner = (p * 2 + 1 - core, lax.axis_index("group"), lax.axis_index("tensor"))
 
     def remote(src, dst, send, recv, device):
@@ -75,8 +76,8 @@
     pl.semaphore_signal(barrier, inc=1, device_id=partner, device_id_type=MESH)
 
     l_copies = [
-        pltpu.make_async_copy(wt_hbm, wt.at[core], w_loc.at[0]),
-        pltpu.make_async_copy(ws_hbm, ws.at[core], w_loc.at[1]),
+        pltpu.make_async_copy(wt_hbm, wt.at[my_rows], w_loc.at[0]),
+        pltpu.make_async_copy(ws_hbm, ws.at[my_rows], w_loc.at[1]),
     ]
     for copy in l_copies:
         copy.start()
@@ -126,8 +127,8 @@
     z_start(8)
 
     w_copies = [
-        remote(wt_hbm, wt.at[core], w_send.at[0], w_recv.at[0], partner),
-        remote(ws_hbm, ws.at[core], w_send.at[1], w_recv.at[1], partner),
+        remote(wt_hbm, wt.at[my_rows], w_send.at[0], w_recv.at[0], partner),
+        remote(ws_hbm, ws.at[my_rows], w_send.at[1], w_recv.at[1], partner),
     ]
     for copy in w_copies:
         copy.start()
@@ -231,12 +232,12 @@
     r0.near()
     r0.column(0)
     r2.begin()
+    r3.begin()
     r1.near()
     r1.column(0)
     r0.far()
     r0.column(-1)
     r0.column(1)
-    r3.begin()
     squares = jnp.zeros((8, tl + sl), F32)
     for k in range(4):
         for j in range(4):
@@ -288,15 +289,14 @@
         v_s = jnp.concatenate([v[:, tl:] for v in pieces], axis=1)
         x_t = (v_t * all_t * gt[:, cut_t]).astype(BF16)
         x_s = (v_s * all_s * gs[:, cut_s]).astype(BF16)
-        for half in range(2):
-            d_t = lax.dot_general(wt[half, :, cut_t], x_t, NT, preferred_element_type=F32)
-            d_s = lax.dot_general(ws[half, :, cut_s], x_s, NT, preferred_element_type=F32)
-            if ring.c == 0:
-                raw_t[half] = d_t
-                raw_s[half] = d_s
-            else:
-                raw_t[half] += d_t
-                raw_s[half] += d_s
+        d_t = lax.dot_general(wt[:, cut_t], x_t, NT, preferred_element_type=F32)
+        d_s = lax.dot_general(ws[:, cut_s], x_s, NT, preferred_element_type=F32)
+        if ring.c == 0:
+            raw_t[...] = d_t
+            raw_s[...] = d_s
+        else:
+            raw_t[...] += d_t
+            raw_s[...] += d_s
 
     r0.finish()
     multiply(r0)
@@ -313,8 +313,9 @@
         vocab0 = ((p * 2 + half) * RZ + z) * vloc
         ids = vocab0 + lax.broadcasted_iota(jnp.int32, (vloc, 128), 0)
         onehot = ids == labels
-        rs = raw_s[half]
-        tan_t = jnp.tanh(raw_t[half] * (1.0 / CAP))
+        part = slice(half * vloc, (half + 1) * vloc)
+        rs = raw_s[part]
+        tan_t = jnp.tanh(raw_t[part] * (1.0 / CAP))
         tan_s = jnp.tanh(rs * (1.0 / CAP))
         log_t = CAP * tan_t
         log_s = CAP * tan_s
@@ -369,23 +370,24 @@
     for half in range(2):
         grad = es_s[half] * scale_s - et_s[half] * scale_t - oh_s[half]
         gbuf[:, half * vloc : (half + 1) * vloc] = grad.T.astype(BF16)
-    part = 512
-    for n in range(ds // part):
-        cut = slice(n * part, (n + 1) * part)
-        term = jnp.dot(
-            gbuf[:, :vloc], ws[0, :, cut], preferred_element_type=F32
-        ) + jnp.dot(gbuf[:, vloc:], ws[1, :, cut], preferred_element_type=F32)
-        obuf[:, :, cut] = term.reshape(PLANE, 8, part).astype(BF16)
-
-    def r_copy(k):
+    dh = ds // 2
+
+    def r_copy(h, k):
         to = (p + k) % PLANE
         return remote(
-            obuf.at[to], rbuf.at[p], r_send.at[0], r_recv.at[0], at_plane(to)
-        )
-
-    @pl.loop(1, PLANE)
-    def _(k):
-        r_copy(k).start()
+            obuf.at[h, to], rbuf.at[h, p], r_send.at[h], r_recv.at[h], at_plane(to)
+        )
+
+    for h in range(2):
+        part = dh // 2
+        for n in range(2):
+            lo = h * dh + n * part
+            term = jnp.dot(gbuf[...], ws[:, lo : lo + part], preferred_element_type=F32)
+            obuf[h, :, :, n * part : (n + 1) * part] = term.reshape(PLANE, 8, part).astype(BF16)
+
+        @pl.loop(1, PLANE)
+        def _(k):
+            r_copy(h, k).start()
 
     loss = cross / sum_t - jnp.log(sum_t) + 2.0 * jnp.log(sum_s) - picked
     radial = scale_s * total[4:5] - scale_t * total[5:6] - total[6:7]
@@ -395,23 +397,27 @@
     out_ref[:, 256:] = pltpu.roll(packed, (128 - p * 8) % 128, 1)
     rad = mine[:, 1:2]
 
-    rbuf[p] = obuf[p]
-
-    await_recv(rbuf.at[pl.ds(0, PLANE - 1)], r_recv.at[0])
-
-    back = jnp.sum(rbuf[...].astype(F32), axis=0) * gs[...]
-    for k in range(RZ):
-        zsend[k, :, :sl] = back[:, k * sl : (k + 1) * sl].astype(BF16)
-
-    def q_copy(k):
-        to = (z + k) % RZ
-        return remote(
-            zsend.at[to], zrecv.at[z], q_send.at[0], q_recv.at[0], at_line(to)
-        )
-
-    @pl.loop(1, RZ)
-    def _(k):
-        q_copy(k).start()
+    for h in range(2):
+        rbuf[h, p] = obuf[h, p]
+
+    def q_start(h, k):
+        to = h * 8 + (z + k) % 8
+
+        @pl.when(to != z)
+        def _():
+            remote(
+                zsend.at[to], zrecv.at[z], q_send.at[0], q_recv.at[0], at_line(to)
+            ).start()
+
+    for h in range(2):
+        await_recv(rbuf.at[h, pl.ds(0, PLANE - 1)], r_recv.at[h])
+        back = jnp.sum(rbuf[h].astype(F32), axis=0) * gs[:, h * dh : (h + 1) * dh]
+        for k in range(8):
+            zsend[h * 8 + k, :, :sl] = back[:, k * sl : (k + 1) * sl].astype(BF16)
+
+        @pl.loop(0, 8)
+        def _(k):
+            q_start(h, k)
 
     await_send(buf.at[0, pl.ds(0, RZ - 1), 0], z_send.at[0])
     await_send(ibuf.at[pl.ds(0, PLANE - 1)], i_send.at[0])
@@ -428,7 +434,8 @@
     out = inv_s * sum_back - (inv_s * inv_s * rad) * sh_ref[...].astype(F32) / ds
     out_ref[:, :sl] = out
 
-    await_send(obuf.at[pl.ds(0, PLANE - 1)], r_send.at[0])
+    for h in range(2):
+        await_send(obuf.at[h, pl.ds(0, PLANE - 1)], r_send.at[h])
     await_send(zsend.at[pl.ds(0, RZ - 1)], q_send.at[0])
 
 
@@ -455,22 +462,22 @@
             pltpu.VMEM((dt // 128, 128), BF16),
             pltpu.VMEM((ds // 128, 128), BF16),
             pltpu.VMEM((2, 128), jnp.int32),
-            pltpu.VMEM((2, vloc, dt), BF16),
-            pltpu.VMEM((2, vloc, ds), BF16),
+            pltpu.VMEM((2 * vloc, dt), BF16),
+            pltpu.VMEM((2 * vloc, ds), BF16),
             pltpu.VMEM((4, PLANE, 4, tok, tl + sl), BF16),
             pltpu.VMEM((PLANE, tok, 128), F32),
             pltpu.VMEM((1, dt), F32),
             pltpu.VMEM((1, ds), F32),
-            pltpu.VMEM((2, vloc, 128), F32),
-            pltpu.VMEM((2, vloc, 128), F32),
+            pltpu.VMEM((2 * vloc, 128), F32),
+            pltpu.VMEM((2 * vloc, 128), F32),
             pltpu.VMEM((2, vloc, 128), F32),
             pltpu.VMEM((2, vloc, 128), F32),
             pltpu.VMEM((2, vloc, 128), F32),
             pltpu.VMEM((PLANE, 8, 128), F32),
             pltpu.VMEM((RZ, 8, 128), F32),
             pltpu.VMEM((128, 2 * vloc), BF16),
-            pltpu.VMEM((PLANE, tok, ds), BF16),
-            pltpu.VMEM((PLANE, tok, ds), BF16),
+            pltpu.VMEM((2, PLANE, tok, ds // 2), BF16),
+            pltpu.VMEM((2, PLANE, tok, ds // 2), BF16),
             pltpu.VMEM((RZ, tok, 256), BF16),
             pltpu.VMEM((RZ, tok, 256), BF16),
             pltpu.VMEM((128, 8), F32),
@@ -480,7 +487,7 @@
             dma((1,)), dma((1,)),
             dma((1,)), dma((1,)),
             dma((1,)), dma((1,)),
-            dma((1,)), dma((1,)),
+            dma((2,)), dma((2,)),
             dma((1,)), dma((1,)),
         ],
         compiler_params=pltpu.CompilerParams(

time: 75.8 us -> 71.2 us (0.939)
  Pallas kernels: 74.9 us -> 70.3 us
    pallas_call x1, Pallas kernels: 73.6 us -> 69 us  [on_device(): pl.pallas_call(kernel, out_shape=jax.ShapeDtypeStruct((tok, 384), F32), i...]
where the time goes in v4:
time: 71.2 us; the launch traced here: 71 us
  Pallas kernels  70.3 us (99%)
    pallas_call x1, Pallas kernels, on_device(): pl.pallas_call(kernel, out_shape=jax.ShapeDtypeStruct((tok, 384), F32), i...  69 us

profile of v4, /device:TPU:32, one launch (start us, length us, event | category | flops | bytes accessed | tf_op | source)
XLA Modules:
  0.0 71.0 jit_solution(8756556876404551603)
XLA Ops:
  0.6 69.0 %shard_map.86.out_ref = f32[8,384]{1,0:T(8,128)} custom-call(bf16[8,288]{1,0:T(8,128)(2,1)} %th_hbm.1, bf16[8,224]{1,0:T(8,128)(2,1)} %sh_hbm.1, bf16[36,128]{1,0:T(8,128)(2,1)} %bitcast.3, bf16[28,128]{1,0:T(8,128)(2,1)} %bitcast.4, s32[2,128]{1,0:T(2,128)} %bitcast.5, bf16[256,4608]{1,0:T(8,128)(2,1)} %wt_hbm.1, bf16[256,3584]{1,0:T(8,128)(2,1)} %ws_hbm.1), custom_call_target="tpu_custom_call" | custom-call | tf_op jit(solution)/shard_map/pallas_call | solution.py:454
  69.7 1.3 %shard_map.87 = (f32[8]{0:T(128)}, bf16[8,224]{1,0:T(8,128)(2,1)}) custom-call(f32[8,384]{1,0:T(8,128)} %shard_map.86.out_ref), custom_call_target="tpu_custom_call" | custom-call | tf_op jit(solution)/shard_map/pallas_call | solution.py:497

commit v5 on v4

--- a/solution.py
+++ b/solution.py
@@ -10,6 +10,7 @@
 MESH = pl.DeviceIdType.MESH
 F32 = jnp.float32
 BF16 = jnp.bfloat16
+PARTS = 4
 RX, RY, RZ = 4, 4, 16
 PLANE = RX * RY
 NT = (((1,), (1,)), ((), ()))
@@ -304,8 +305,8 @@
     r1.finish()
     multiply(r1)
     r2.finish()
+    r3.finish()
     multiply(r2)
-    r3.finish()
     multiply(r3)
 
     sums = [jnp.zeros((1, 128), F32) for _ in range(7)]
@@ -370,7 +371,7 @@
     for half in range(2):
         grad = es_s[half] * scale_s - et_s[half] * scale_t - oh_s[half]
         gbuf[:, half * vloc : (half + 1) * vloc] = grad.T.astype(BF16)
-    dh = ds // 2
+    dh = ds // PARTS
 
     def r_copy(h, k):
         to = (p + k) % PLANE
@@ -378,12 +379,11 @@
             obuf.at[h, to], rbuf.at[h, p], r_send.at[h], r_recv.at[h], at_plane(to)
         )
 
-    for h in range(2):
-        part = dh // 2
-        for n in range(2):
-            lo = h * dh + n * part
-            term = jnp.dot(gbuf[...], ws[:, lo : lo + part], preferred_element_type=F32)
-            obuf[h, :, :, n * part : (n + 1) * part] = term.reshape(PLANE, 8, part).astype(BF16)
+    for h in range(PARTS):
+        term = jnp.dot(
+            gbuf[...], ws[:, h * dh : (h + 1) * dh], preferred_element_type=F32
+        )
+        obuf[h] = term.reshape(PLANE, 8, dh).astype(BF16)
 
         @pl.loop(1, PLANE)
         def _(k):
@@ -397,11 +397,11 @@
     out_ref[:, 256:] = pltpu.roll(packed, (128 - p * 8) % 128, 1)
     rad = mine[:, 1:2]
 
-    for h in range(2):
+    for h in range(PARTS):
         rbuf[h, p] = obuf[h, p]
 
     def q_start(h, k):
-        to = h * 8 + (z + k) % 8
+        to = h * (RZ // PARTS) + (z + k) % (RZ // PARTS)
 
         @pl.when(to != z)
         def _():
@@ -409,13 +409,13 @@
                 zsend.at[to], zrecv.at[z], q_send.at[0], q_recv.at[0], at_line(to)
             ).start()
 
-    for h in range(2):
+    for h in range(PARTS):
         await_recv(rbuf.at[h, pl.ds(0, PLANE - 1)], r_recv.at[h])
         back = jnp.sum(rbuf[h].astype(F32), axis=0) * gs[:, h * dh : (h + 1) * dh]
-        for k in range(8):
-            zsend[h * 8 + k, :, :sl] = back[:, k * sl : (k + 1) * sl].astype(BF16)
-
-        @pl.loop(0, 8)
+        for k in range(RZ // PARTS):
+            zsend[h * (RZ // PARTS) + k, :, :sl] = back[:, k * sl : (k + 1) * sl].astype(BF16)
+
+        @pl.loop(0, RZ // PARTS)
         def _(k):
             q_start(h, k)
 
@@ -434,7 +434,7 @@
     out = inv_s * sum_back - (inv_s * inv_s * rad) * sh_ref[...].astype(F32) / ds
     out_ref[:, :sl] = out
 
-    for h in range(2):
+    for h in range(PARTS):
         await_send(obuf.at[h, pl.ds(0, PLANE - 1)], r_send.at[h])
     await_send(zsend.at[pl.ds(0, RZ - 1)], q_send.at[0])
 
@@ -476,8 +476,8 @@
             pltpu.VMEM((PLANE, 8, 128), F32),
             pltpu.VMEM((RZ, 8, 128), F32),
             pltpu.VMEM((128, 2 * vloc), BF16),
-            pltpu.VMEM((2, PLANE, tok, ds // 2), BF16),
-            pltpu.VMEM((2, PLANE, tok, ds // 2), BF16),
+            pltpu.VMEM((PARTS, PLANE, tok, ds // PARTS), BF16),
+            pltpu.VMEM((PARTS, PLANE, tok, ds // PARTS), BF16),
             pltpu.VMEM((RZ, tok, 256), BF16),
             pltpu.VMEM((RZ, tok, 256), BF16),
             pltpu.VMEM((128, 8), F32),
@@ -487,7 +487,7 @@
             dma((1,)), dma((1,)),
             dma((1,)), dma((1,)),
             dma((1,)), dma((1,)),
-            dma((2,)), dma((2,)),
+            dma((PARTS,)), dma((PARTS,)),
             dma((1,)), dma((1,)),
         ],
         compiler_params=pltpu.CompilerParams(

time: 71.2 us -> 70.2 us (0.986)
  Pallas kernels: 70.3 us -> 69.3 us
    pallas_call x1, Pallas kernels: 69 us -> 68 us  [on_device(): pl.pallas_call(kernel, out_shape=jax.ShapeDtypeStruct((tok, 384), F32), i...]
where the time goes in v5:
time: 70.2 us; the launch traced here: 69.9 us
  Pallas kernels  69.3 us (99%)
    pallas_call x1, Pallas kernels, on_device(): pl.pallas_call(kernel, out_shape=jax.ShapeDtypeStruct((tok, 384), F32), i...  68 us

profile of v5, /device:TPU:32, one launch (start us, length us, event | category | flops | bytes accessed | tf_op | source)
XLA Modules:
  0.0 69.9 jit_solution(6021521248688461496)
XLA Ops:
  0.6 68.0 %shard_map.86.out_ref = f32[8,384]{1,0:T(8,128)} custom-call(bf16[8,288]{1,0:T(8,128)(2,1)} %th_hbm.1, bf16[8,224]{1,0:T(8,128)(2,1)} %sh_hbm.1, bf16[36,128]{1,0:T(8,128)(2,1)} %bitcast.3, bf16[28,128]{1,0:T(8,128)(2,1)} %bitcast.4, s32[2,128]{1,0:T(2,128)} %bitcast.5, bf16[256,4608]{1,0:T(8,128)(2,1)} %wt_hbm.1, bf16[256,3584]{1,0:T(8,128)(2,1)} %ws_hbm.1), custom_call_target="tpu_custom_call" | custom-call | tf_op jit(solution)/shard_map/pallas_call | solution.py:454
  68.6 1.3 %shard_map.87 = (f32[8]{0:T(128)}, bf16[8,224]{1,0:T(8,128)(2,1)}) custom-call(f32[8,384]{1,0:T(8,128)} %shard_map.86.out_ref), custom_call_target="tpu_custom_call" | custom-call | tf_op jit(solution)/shard_map/pallas_call | solution.py:497

commit v6 on v5

--- a/solution.py
+++ b/solution.py
@@ -453,7 +453,7 @@
     dma = pltpu.SemaphoreType.DMA
     out = pl.pallas_call(
         kernel,
-        out_shape=jax.ShapeDtypeStruct((tok, 384), F32),
+        out_shape=pltpu.VMEM((tok, 384), F32),
         in_specs=[hbm] * 7,
         out_specs=vmem,
         scratch_shapes=[
@@ -501,7 +501,7 @@
         ),
         in_specs=[vmem],
         out_specs=(vmem, vmem),
-    )(out)
+    )(pltpu.with_memory_space_constraint(out, pltpu.VMEM))
 
 
 def solution(mesh):

time: 70.2 us -> 68.8 us (0.980)
  Pallas kernels: 69.3 us -> 68 us
    pallas_call x1, Pallas kernels: 1.31 us -> 0.6 us  [on_device(): pl.pallas_call(unpack, out_shape=(jax.ShapeDtypeStruct((tok,), F32), jax....]
where the time goes in v6:
time: 68.8 us; the launch traced here: 68.6 us
  Pallas kernels  68 us (99%)
    pallas_call x1, Pallas kernels, on_device(): pl.pallas_call(kernel, out_shape=pltpu.VMEM((tok, 384), F32), in_specs=[h...  67.4 us

profile of v6, /device:TPU:32, one launch (start us, length us, event | category | flops | bytes accessed | tf_op | source)
XLA Modules:
  0.0 68.6 jit_solution(4841000944766359248)
XLA Ops:
  0.6 67.4 %shard_map.86.out_ref = f32[8,384]{1,0:T(8,128)S(1)} custom-call(bf16[8,288]{1,0:T(8,128)(2,1)} %th_hbm.1, bf16[8,224]{1,0:T(8,128)(2,1)} %sh_hbm.1, bf16[36,128]{1,0:T(8,128)(2,1)} %bitcast.3, bf16[28,128]{1,0:T(8,128)(2,1)} %bitcast.4, s32[2,128]{1,0:T(2,128)} %bitcast.5, bf16[256,4608]{1,0:T(8,128)(2,1)} %wt_hbm.1, bf16[256,3584]{1,0:T(8,128)(2,1)} %ws_hbm.1), custom_call_target="tpu_custom_call" | custom-call | tf_op jit(solution)/shard_map/pallas_call | solution.py:454
  68.0 0.6 shard_map.87

commit v7 on v6

--- a/solution.py
+++ b/solution.py
@@ -357,8 +357,7 @@
 
     sz[z] = jnp.sum(sxy[...], axis=0)
 
-    @pl.loop(1, RZ)
-    def _(k):
+    for k in (8, 7, 9, 6, 10, 5, 11, 4, 12, 3, 13, 2, 14, 1, 15):
         b_copy(k).start()
 
     await_recv(sz.at[pl.ds(0, RZ - 1)], b_recv.at[0])

time: 68.8 us -> 68.4 us (level)
  no operation moved by 1% of the time
where the time goes in v7:
time: 68.4 us; the launch traced here: 68.3 us
  Pallas kernels  67.6 us (99%)
    pallas_call x1, Pallas kernels, on_device(): pl.pallas_call(kernel, out_shape=pltpu.VMEM((tok, 384), F32), in_specs=[h...  67 us

profile of v7, /device:TPU:32, one launch (start us, length us, event | category | flops | bytes accessed | tf_op | source)
XLA Modules:
  0.0 68.3 jit_solution(2601202314305149352)
XLA Ops:
  0.6 67.0 %shard_map.86.out_ref = f32[8,384]{1,0:T(8,128)S(1)} custom-call(bf16[8,288]{1,0:T(8,128)(2,1)} %th_hbm.1, bf16[8,224]{1,0:T(8,128)(2,1)} %sh_hbm.1, bf16[36,128]{1,0:T(8,128)(2,1)} %bitcast.3, bf16[28,128]{1,0:T(8,128)(2,1)} %bitcast.4, s32[2,128]{1,0:T(2,128)} %bitcast.5, bf16[256,4608]{1,0:T(8,128)(2,1)} %wt_hbm.1, bf16[256,3584]{1,0:T(8,128)(2,1)} %ws_hbm.1), custom_call_target="tpu_custom_call" | custom-call | tf_op jit(solution)/shard_map/pallas_call | solution.py:453
  67.7 0.6 shard_map.87

commit v8 on v7

--- a/solution.py
+++ b/solution.py
@@ -131,9 +131,6 @@
         remote(wt_hbm, wt.at[my_rows], w_send.at[0], w_recv.at[0], partner),
         remote(ws_hbm, ws.at[my_rows], w_send.at[1], w_recv.at[1], partner),
     ]
-    for copy in w_copies:
-        copy.start()
-
     class Ring:
         def __init__(self, c, delta, x_first, way):
             self.c, self.q, self.delta = c, (quad + delta) % 4, delta
@@ -229,6 +226,9 @@
         Ring(2, 4 - beside, True, -1), TwoStep(3, 2, False, -1),
     ]
     r0.begin()
+    for copy in w_copies:
+        copy.start()
+
     r1.begin()
     r0.near()
     r0.column(0)

time: 68.4 us -> 68.4 us (level)
  no operation moved by 1% of the time
where the time goes in v8:
time: 68.4 us; the launch traced here: 68.3 us
  Pallas kernels  67.6 us (99%)
    pallas_call x1, Pallas kernels, on_device(): pl.pallas_call(kernel, out_shape=pltpu.VMEM((tok, 384), F32), in_specs=[h...  67 us

profile of v8, /device:TPU:32, one launch (start us, length us, event | category | flops | bytes accessed | tf_op | source)
XLA Modules:
  0.0 68.3 jit_solution(17369041286395974752)
XLA Ops:
  0.6 67.0 %shard_map.86.out_ref = f32[8,384]{1,0:T(8,128)S(1)} custom-call(bf16[8,288]{1,0:T(8,128)(2,1)} %th_hbm.1, bf16[8,224]{1,0:T(8,128)(2,1)} %sh_hbm.1, bf16[36,128]{1,0:T(8,128)(2,1)} %bitcast.3, bf16[28,128]{1,0:T(8,128)(2,1)} %bitcast.4, s32[2,128]{1,0:T(2,128)} %bitcast.5, bf16[256,4608]{1,0:T(8,128)(2,1)} %wt_hbm.1, bf16[256,3584]{1,0:T(8,128)(2,1)} %ws_hbm.1), custom_call_target="tpu_custom_call" | custom-call | tf_op jit(solution)/shard_map/pallas_call | solution.py:453
  67.7 0.6 shard_map.87
